TPU v7x, 256 devices: a whole 4x4x8 slice. The times are simulated.
256 devices in a mesh: pop: 16 (over z_hi, x, core), dp: 16 (over z_lo, y).
Axes of the slice: x: 4, y: 4, z: 8 (z_hi: 2, z_lo: 4; z = z_hi * 4 + z_lo), core: 2. Of those that a mesh axis runs over, the one named last changes fastest.
Arguments:
- state_pool: bfloat16 [16384, 2048], P('dp'), may hold values from -6 to 6
- probe_row: int32 [16384], P('dp'), may hold values from 0 to 1023
- action: int32 [16384], P('dp'), may hold values from 0 to 17
- w_hidden: bfloat16 [16, 2048, 1024], P('pop'), may hold values from -0.125 to 0.125
- w_head: bfloat16 [16, 18, 1024], P('pop'), may hold values from -0.1875 to 0.1875
- targets: float32 [16, 16384], P('pop', 'dp'), may hold values from -6 to 6
Outputs:
- grad_hidden: float32 [16, 2048, 1024], P('pop', 'dp')
- grad_head: float32 [16, 18, 1024], P('pop', None, 'dp')
All inputs are finite; a program needn't handle non-finite values.
Results may differ from a plain program's by a relative error of at most 0.013.
Values sent between devices are 32-bit elements; how exact they have to be, the bound alone decides.
No kernel may reach another device: no remote copies, remote signals or barrier semaphores. Data moves between devices by JAX's collectives and lax.ppermute only.
A program may use at most 128 MiB of HBM per device.

v0:
```python
import functools
import math

import jax
import jax.numpy as jnp
from jax import lax
from jax.experimental import pallas as pl
from jax.experimental.pallas import tpu as pltpu
from jax.sharding import PartitionSpec as P

HID = 1024
ACTIONS = 18
PAD = 32
CHUNKS = (80, 48)
EXTRA = 8
SHARES = (0, 2, 4, 6, 1, 3, 5, 7)
STEPS = [(y, z) for y in (2, 1, 3, 0) for z in (0, 3, 1, 2)]
F32 = jnp.float32
BF16 = jnp.bfloat16
NT = (((1,), (1,)), ((), ()))
TN = (((0,), (0,)), ((), ()))
VMEM_SPEC = pl.BlockSpec(memory_space=pltpu.VMEM)
HBM_SPEC = pl.BlockSpec(memory_space=pltpu.HBM)


def params(mib):
    return pltpu.CompilerParams(vmem_limit_bytes=mib * 1024 * 1024)


def cost(us):
    return pl.CostEstimate(flops=int(us * 1.1e9), bytes_accessed=0, transcendentals=0)


def after(value, *first):
    return lax.optimization_barrier((value, first))[0]


def spot():
    place = lax.axis_index("dp")
    return place // 4, place % 4, lax.axis_index("pop") % len(SHARES)


def block_of(z, y, i):
    step_y, step_z = STEPS[i]
    return (z ^ step_z) * 4 + (y + step_y) % 4


def turn(rows_ref, turned_ref, z, y, blocks):
    width = turned_ref.shape[1]
    for i in blocks:
        start = pl.multiple_of(block_of(z, y, i) * width, width)
        turned_ref[i] = rows_ref[:, pl.ds(start, width)].T


def padded(head_ref, wide_ref):
    wide_ref[...] = jnp.zeros_like(wide_ref)
    wide_ref[0:ACTIONS, :] = head_ref[0].astype(F32)


def split3(v):
    hi = v.astype(BF16)
    rest = v - hi.astype(F32)
    mid = rest.astype(BF16)
    low = (rest - mid.astype(F32)).astype(BF16)
    return jnp.concatenate([hi, mid, low], axis=0)


def join3(v):
    return v[:PAD] + v[PAD : 2 * PAD] + v[2 * PAD :]


def row_onehot(start, size, row):
    ids = lax.broadcasted_iota(jnp.int32, (size, row.shape[1]), 0) + start
    return jnp.where(ids == row, 1.0, 0.0).astype(BF16)


def sigmoid(v):
    return 0.5 * jnp.tanh(0.5 * v) + 0.5


def forward_kernel(
    pool_hbm, w_hbm, head_ref, row_ref, act_ref, target_ref, hid_ref, slope_ref, turned_ref, emb_ref, facts_ref,
    acc_ref, pool_ref, w_ref, wide_ref, sems,
):
    z, y, _ = spot()
    rows, hidden = hid_ref.shape
    tile, width = rows // 2, hidden // 2
    row_of = lambda i: pl.ds(i * tile, tile)
    pools = [pltpu.make_async_copy(pool_hbm.at[row_of(i), :], pool_ref.at[row_of(i), :], sems.at[i]) for i in range(2)]
    halves = [
        pltpu.make_async_copy(w_hbm.at[0, :, pl.ds(j * width, width)], w_ref.at[j], sems.at[2 + j]) for j in range(2)
    ]
    for copy in (pools[0], halves[0], halves[1], pools[1]):
        copy.start()
    padded(head_ref, wide_ref)
    facts_ref[0:1, :] = target_ref[...]
    facts_ref[1:2, :] = row_ref[...].astype(F32)
    facts_ref[2:3, :] = act_ref[...].astype(F32)
    facts_ref[3:, :] = jnp.zeros((facts_ref.shape[0] - 3, facts_ref.shape[1]), F32)
    pools[0].wait()
    for i in range(2):
        if i == 1:
            pools[1].wait()
        for j in range(2):
            if i == 0:
                halves[j].wait()
            columns = slice(j * width, (j + 1) * width)
            v = jnp.dot(pool_ref[row_of(i), :], w_ref[j], preferred_element_type=F32)
            sig = sigmoid(v)
            hid = (v * sig).astype(BF16)
            hid_ref[row_of(i), columns] = hid

            @pl.when(z // 2 == j)
            def _():
                slope_ref[row_of(i), :] = sig * (1.0 + v * (1.0 - sig))

            logits = lax.dot_general(wide_ref[:, columns].astype(BF16), hid, NT, preferred_element_type=F32)
            if j == 0:
                acc_ref[:, row_of(i)] = logits
            else:
                acc_ref[:, row_of(i)] += logits
                if i == 1:
                    turn(pool_ref, turned_ref, z, y, range(turned_ref.shape[0]))
    logits = acc_ref[...]
    parts = split3(logits - jnp.sum(logits, axis=0, keepdims=True) / ACTIONS)
    picked = jnp.zeros((3 * PAD, row_ref.shape[1]), F32)
    for i in range(0, rows, 256):
        picked += jnp.dot(parts[:, i : i + 256], row_onehot(i, 256, row_ref[...]), preferred_element_type=F32)
    chosen = lax.broadcasted_iota(jnp.int32, (PAD, row_ref.shape[1]), 0) == act_ref[...]
    emb_ref[...] = jnp.sum(jnp.where(chosen, join3(picked), 0.0), axis=0, keepdims=True)


def forward(pool, w, head, row, act, target):
    rows, feat = pool.shape
    hid = w.shape[2]
    probes = row.shape[1]
    blocks = len(STEPS)
    return pl.pallas_call(
        forward_kernel,
        in_specs=[HBM_SPEC] * 2 + [VMEM_SPEC] * 4,
        out_specs=[VMEM_SPEC] * 5,
        out_shape=[
            jax.ShapeDtypeStruct((rows, hid), BF16),
            jax.ShapeDtypeStruct((rows, hid // 2), F32),
            jax.ShapeDtypeStruct((blocks, feat // blocks, rows), BF16),
            jax.ShapeDtypeStruct((1, probes), F32),
            jax.ShapeDtypeStruct((8, probes), F32),
        ],
        scratch_shapes=[
            pltpu.VMEM((PAD, rows), F32),
            pltpu.VMEM((rows, feat), BF16),
            pltpu.VMEM((2, feat, hid // 2), BF16),
            pltpu.VMEM((PAD, hid), F32),
            pltpu.SemaphoreType.DMA((4,)),
        ],
        compiler_params=params(42),
        cost_estimate=cost(0.3),
        name="forward",
    )(pool, w, head, row, act, target)


def distance_kernel(near_ref, far_ref, facts_ref, out_ref, pack_ref):
    pop = jnp.concatenate([near_ref[...], far_ref[...]], axis=0)
    agents = pop.shape[0]
    lanes = lax.broadcasted_iota(jnp.int32, (agents, 128), 1)
    total = jnp.zeros((agents, 128), F32)
    for i in range(agents):
        gap = pop - pop[i : i + 1, :]
        total = jnp.where(lanes == i, jnp.sum(gap * gap, axis=1, keepdims=True), total)
    out_ref[...] = total
    pack_ref[0:agents, :] = pop
    pack_ref[agents:, :] = facts_ref[...]


def distance_parts(near, far, facts):
    agents, probes = 2 * near.shape[0], near.shape[1]
    return pl.pallas_call(
        distance_kernel,
        in_specs=[VMEM_SPEC] * 3,
        out_specs=[VMEM_SPEC] * 2,
        out_shape=[
            jax.ShapeDtypeStruct((agents, 128), F32),
            jax.ShapeDtypeStruct((agents + facts.shape[0], probes), F32),
        ],
        compiler_params=params(16),
        cost_estimate=cost(0.2),
        name="distances",
    )(near, far, facts)


def partner_rows(z, y, share_refs, w_hbm, turned_ref, rows_ref, w_ref, sem):
    share, width = share_refs[0].shape[0], w_ref.shape[1]
    columns = pl.ds(pl.multiple_of(z // 2 * width, width), width)
    copy = pltpu.make_async_copy(w_hbm.at[0, :, columns], w_ref, sem)
    copy.start()
    for j, ref in enumerate(share_refs):
        rows_ref[pl.ds(j * share, share), :] = ref[...].astype(BF16)
    copy.wait()
    v = jnp.dot(rows_ref[...], w_ref[...], preferred_element_type=F32)
    turn(rows_ref, turned_ref, z, y, range(turned_ref.shape[0]))
    sig = sigmoid(v)
    return sig * (1.0 + v * (1.0 - sig))


def marked_sums(marked, hot):
    return join3(lax.dot_general(marked, hot, NT, preferred_element_type=F32))


def scaled(sums, cents, slope):
    part_hi = sums.astype(BF16)
    part_lo = (sums - part_hi.astype(F32)).astype(BF16)
    stacked = jnp.concatenate([part_hi, part_hi, part_lo], axis=0)
    return (lax.dot_general(stacked, cents, TN, preferred_element_type=F32) * slope).astype(BF16)


def partner_hot(where, first, share, row):
    return jnp.concatenate([row_onehot((where ^ SHARES[j]) * share, share, row) for j in (first, first + 1)], axis=0)


def partner_a_kernel(a_ref, b_ref, c_ref, d_ref, w_hbm, slope_ref, turned_ref, rows_ref, w_ref, sem):
    z, y, _ = spot()
    slope_ref[...] = partner_rows(z, y, (a_ref, b_ref, c_ref, d_ref), w_hbm, turned_ref, rows_ref, w_ref, sem)


def partner_b_kernel(
    a_ref, b_ref, c_ref, d_ref, w_hbm, marked_ref, cents_ref, pack_ref, dz_ref, turned_ref, rows_ref, w_ref, sem
):
    z, y, where = spot()
    share = a_ref.shape[0]
    slope = partner_rows(z, y, (a_ref, b_ref, c_ref, d_ref), w_hbm, turned_ref, rows_ref, w_ref, sem)
    row = pack_ref[17:18, :].astype(jnp.int32)
    for i in range(2):
        here = slice(2 * i * share, 2 * (i + 1) * share)
        sums = marked_sums(marked_ref[...], partner_hot(where, 4 + 2 * i, share, row))
        dz_ref[here, :] = scaled(sums, cents_ref[...], slope[here])


def partner_part(shares, w, more=()):
    share, feat = shares[0].shape
    half = w.shape[2] // 2
    blocks = len(STEPS)
    return pl.pallas_call(
        partner_b_kernel if more else partner_a_kernel,
        in_specs=[VMEM_SPEC] * 4 + [HBM_SPEC] + [VMEM_SPEC] * len(more),
        out_specs=[VMEM_SPEC] * 2,
        out_shape=[
            jax.ShapeDtypeStruct((4 * share, half), BF16 if more else F32),
            jax.ShapeDtypeStruct((blocks, feat // blocks, 4 * share), BF16),
        ],
        scratch_shapes=[
            pltpu.VMEM((4 * share, feat), BF16),
            pltpu.VMEM((feat, half), BF16),
            pltpu.SemaphoreType.DMA(()),
        ],
        compiler_params=params(16),
        cost_estimate=cost(0.3),
        name="partner",
    )(*shares, w, *more)


def coeff_kernel(
    total_probes, scaling, d0, d1, near_ref, far_ref, facts_ref, pack_ref, head_ref, slope_a_ref, slope_ref, hid_ref,
    dz_ref, heads_ref, marked_ref, cents_ref, sums_ref, wide_ref, ghead_ref,
):
    z, y, where = spot()
    width = slope_ref.shape[1]
    columns = pl.ds(pl.multiple_of(z // 2 * width, width), width)
    padded(head_ref, wide_ref)
    pop = jnp.concatenate([near_ref[...], far_ref[...]], axis=0)
    agents = pop.shape[0]
    pop2 = pack_ref[0:agents, :]
    row, act = facts_ref[1:2, :].astype(jnp.int32), facts_ref[2:3, :].astype(jnp.int32)
    row2 = pack_ref[agents + 1 : agents + 2, :].astype(jnp.int32)
    act2 = pack_ref[agents + 2 : agents + 3, :].astype(jnp.int32)
    lanes = lax.broadcasted_iota(jnp.int32, (agents, 128), 1)
    subs = lax.broadcasted_iota(jnp.int32, (agents, 128), 0)
    kern = jnp.exp(-(d0[...] + d1[...]) / total_probes)
    system = jnp.where(lanes < agents, kern, jnp.where((lanes == agents) & (subs == 0), 1.0, 0.0))
    for k in range(agents):
        pivot_row = system[k : k + 1, :] / system[k : k + 1, k : k + 1]
        system = jnp.where(subs == k, pivot_row, system - system[:, k : k + 1] * pivot_row)
    mix = system[:, agents : agents + 1] * kern[:, 0:1]

    def marked(people, target, act):
        emb = people[0:1, :]
        pulled = jnp.sum(mix * people, axis=0, keepdims=True)
        diverse = 2.0 * (jnp.sum(mix, axis=0, keepdims=True) * emb - pulled)
        coeff = scaling * (emb - target) + scaling * diverse
        chosen = lax.broadcasted_iota(jnp.int32, (PAD, act.shape[1]), 0) == act
        return split3(jnp.where(chosen, coeff, 0.0))

    head = wide_ref[:, columns]
    centered = head - jnp.sum(head, axis=0, keepdims=True) / ACTIONS
    cent_hi = centered.astype(BF16)
    cent_lo = (centered - cent_hi.astype(F32)).astype(BF16)
    cents = jnp.concatenate([cent_hi, cent_lo, cent_hi], axis=0)

    rows = slope_ref.shape[0]
    tile = 256
    mine = marked(pop, facts_ref[0:1, :], act)
    theirs = marked(pop2, pack_ref[agents : agents + 1, :], act2)
    marked_ref[...] = theirs
    cents_ref[...] = cents
    for i in range(rows // tile):
        here = pl.ds(i * tile, tile)
        sums = marked_sums(mine, row_onehot(i * tile, tile, row))
        sums_ref[:, here] = sums
        dz_ref[here, :] = scaled(sums, cents, slope_ref[here, :])
    share = tile // 2
    for i in range(slope_a_ref.shape[0] // tile):
        sums = marked_sums(theirs, partner_hot(where, 2 * i, share, row2))
        dz_ref[pl.ds(rows + i * tile, tile), :] = scaled(sums, cents, slope_a_ref[pl.ds(i * tile, tile), :])
    sums = sums_ref[...]
    even = split3(sums - jnp.sum(sums, axis=0, keepdims=True) / ACTIONS)
    ghead_ref[...] = join3(jnp.dot(even, hid_ref[...], preferred_element_type=F32))
    blocks = heads_ref.shape[0]
    cols = ghead_ref.shape[1] // blocks
    for i in range(blocks):
        place = block_of(z, y, i)
        pair = ghead_ref[:, pl.ds(pl.multiple_of(place // 2 * 2 * cols, 2 * cols), 2 * cols)]
        mine = jnp.where(place % 2 == 0, pair[:, :cols], pair[:, cols:])
        laid = [mine[g * EXTRA : (g + 1) * EXTRA] for g in range(3)]
        rest = jnp.zeros((EXTRA, heads_ref.shape[2] - 3 * cols), F32)
        heads_ref[i] = jnp.concatenate(laid + [rest], axis=1)


def coefficients(total_probes, dists, near, far, facts, pack, head, slope_a, slope, hid):
    rows, width = hid.shape
    half = width // 2
    scaling = math.sqrt(HID / total_probes)
    return pl.pallas_call(
        functools.partial(coeff_kernel, total_probes, scaling),
        in_specs=[VMEM_SPEC] * 10,
        out_specs=[VMEM_SPEC] * 4,
        out_shape=[
            jax.ShapeDtypeStruct((rows + slope_a.shape[0], half), BF16),
            jax.ShapeDtypeStruct((len(STEPS), EXTRA, half), F32),
            jax.ShapeDtypeStruct((3 * PAD, rows), BF16),
            jax.ShapeDtypeStruct((3 * PAD, half), BF16),
        ],
        scratch_shapes=[
            pltpu.VMEM((PAD, rows), F32),
            pltpu.VMEM((PAD, width), F32),
            pltpu.VMEM((PAD, width), F32),
        ],
        compiler_params=params(16),
        cost_estimate=cost(0.3),
        name="coefficients",
    )(*dists, near, far, facts, pack, head, slope_a, slope, hid)


def grad_kernel(plan, *refs):
    own_ref, a_ref, b_ref, dz_ref, dz_b_ref, heads_ref = refs[:6]
    mine, part = own_ref.shape[2], a_ref.shape[2]
    width = dz_ref.shape[1]
    products = ((own_ref, dz_ref, 0, mine), (a_ref, dz_ref, mine, part), (b_ref, dz_b_ref, 0, part))
    for blocks, begin, end, outs, more in plan:
        rows = end - begin
        total = jnp.zeros((2 * rows, width), F32)
        for ref, right_ref, start, depth in products:
            left = jnp.concatenate([ref[i, begin:end, :] for i in blocks], axis=0)
            total += jnp.dot(left, right_ref[start : start + depth, :], preferred_element_type=F32)
        for q, block in enumerate(blocks):
            for out, at, size, extra in outs:
                out_ref, slot = refs[out[q][0]], out[q][1]
                value = total[q * rows + at : q * rows + at + size]
                heads = heads_ref[block] if extra else None
                if more is not None:
                    add_ref, add_slot = refs[more[q][0]], more[q][1]
                    value = value + add_ref[add_slot, 0:size, :]
                    heads = heads + add_ref[add_slot, size:, :] if extra else None
                out_ref[slot, 0:size, :] = value
                if extra:
                    out_ref[slot, size:, :] = heads


def gradient(parts, groups, which, more=None):
    dz = parts[3]
    width = dz.shape[1]
    chunks = [(sum(CHUNKS[:c]), CHUNKS[c], c == len(CHUNKS) - 1) for c in which]
    begin, end = chunks[0][0], chunks[-1][0] + chunks[-1][1]
    shapes = [
        jax.ShapeDtypeStruct((len(group), size + (EXTRA if extra else 0), width), F32)
        for group in groups
        for _, size, extra in chunks
    ]
    extras = [] if more is None else [more]
    first = len(parts) + len(extras)
    places = [(block, g, slot) for g, group in enumerate(groups) for slot, block in enumerate(group)]
    plan = []
    for k in range(0, len(places), 2):
        pair = places[k : k + 2]
        outs = [
            ([(first + g * len(chunks) + c, slot) for _, g, slot in pair], at - begin, size, extra)
            for c, (at, size, extra) in enumerate(chunks)
        ]
        added = None if more is None else [(len(parts), k), (len(parts), k + 1)]
        plan.append(([block for block, _, _ in pair], begin, end, outs, added))
    outs = pl.pallas_call(
        functools.partial(grad_kernel, plan),
        in_specs=[VMEM_SPEC] * first,
        out_specs=[VMEM_SPEC] * len(shapes),
        out_shape=shapes,
        compiler_params=params(16),
        cost_estimate=cost(0.3),
        name="gradient",
    )(*parts, *extras)
    return [outs[i : i + len(chunks)] for i in range(0, len(outs), len(chunks))]


def add_kernel(at, into_ref, more_ref, out_ref):
    here = slice(at, at + more_ref.shape[0])
    out_ref[here] = into_ref[here] + more_ref[...]


def add_into(into, more, at):
    return pl.pallas_call(
        functools.partial(add_kernel, at),
        in_specs=[VMEM_SPEC] * 2,
        out_specs=VMEM_SPEC,
        out_shape=jax.ShapeDtypeStruct(into.shape, F32),
        input_output_aliases={0: 0},
        compiler_params=params(16),
        cost_estimate=cost(0.1),
        name="add_into",
    )(into, more)


def fold_kernel(count, *refs):
    at = 0
    for out_ref in refs[count:]:
        size = out_ref.shape[0]
        out_ref[...] = sum((ref[at : at + size] for ref in refs[1:count]), refs[0][at : at + size])
        at += size


def fold(terms, per):
    blocks = terms[0].shape[0] // per
    return pl.pallas_call(
        functools.partial(fold_kernel, len(terms)),
        in_specs=[VMEM_SPEC] * len(terms),
        out_specs=[VMEM_SPEC] * blocks,
        out_shape=[jax.ShapeDtypeStruct((per, *terms[0].shape[1:]), F32)] * blocks,
        compiler_params=params(16),
        cost_estimate=cost(0.1),
        name="fold",
    )(*terms)


def finish_kernel(*refs):
    out_ref, two_ref = refs[-2:]
    z, _, _ = spot()
    width = refs[0].shape[2]
    left = pl.ds(pl.multiple_of(z // 2 * width, width), width)
    right = pl.ds(pl.multiple_of((1 - z // 2) * width, width), width)
    at = 0
    for c, size in enumerate(CHUNKS):
        own, other = refs[2 * c : 2 * c + 2]
        out_ref[0, at : at + size, left] = own[0, 0:size, :]
        out_ref[0, at : at + size, right] = other[0, 0:size, :]
        at += size
    heads = own[0, CHUNKS[-1] :, :] + other[0, CHUNKS[-1] :, :]
    cols = two_ref.shape[2]
    for g in range(3):
        count = min(EXTRA, ACTIONS - g * EXTRA)
        two_ref[g * EXTRA : g * EXTRA + count] = heads[0:count, g * cols : (g + 1) * cols].reshape(count, 1, cols)


def finish(pieces, cols):
    rows, width = sum(CHUNKS), pieces[0].shape[2]
    return pl.pallas_call(
        finish_kernel,
        grid=(1,),
        in_specs=[VMEM_SPEC] * len(pieces),
        out_specs=[
            pl.BlockSpec((1, rows, 2 * width), lambda i: (0, 0, 0)),
            pl.BlockSpec((ACTIONS, 1, cols), lambda i: (0, 0, 0)),
        ],
        out_shape=[
            jax.ShapeDtypeStruct((1, rows, 2 * width), F32),
            jax.ShapeDtypeStruct((ACTIONS, 1, cols), F32),
        ],
        compiler_params=params(16),
        cost_estimate=cost(0.1),
        name="finish",
    )(*pieces)


def shift_y(v, s):
    return lax.ppermute(v, "dp", [(z * 4 + y, z * 4 + (y + s) % 4) for z in range(4) for y in range(4)])


def swap(v, axis, mask):
    return lax.ppermute(v, axis, [(i, i ^ mask) for i in range(16)])


def to_partner_rows(v):
    return lax.ppermute(
        v,
        ("pop", "dp"),
        [(p * 16 + d, (p ^ (8 if d // 4 in (0, 3) else 0)) * 16 + (d ^ 12)) for p in range(16) for d in range(16)],
    )


def body(state_pool, probe_row, action, w_hidden, w_head, targets):
    probes = probe_row.shape[0]
    total_probes = probes * lax.axis_size("dp")
    share = state_pool.shape[0] // len(SHARES)
    row = probe_row.reshape(1, probes)
    act = action.reshape(1, probes)

    _, _, where = spot()
    cut = lambda i: lax.dynamic_slice_in_dim(state_pool, i * share, share, 0).astype(F32)
    share0 = to_partner_rows(cut(where))
    next_share = cut(where ^ 4)

    hid, slope, turned, near, facts = forward(state_pool, w_hidden, w_head, row, act, targets)
    for mask in (1, 2, 4):
        near = jnp.concatenate([near, swap(near, "pop", mask)], axis=0)
    far = swap(near, "pop", 8)
    share4 = to_partner_rows(after(next_share, far))
    share0 = after(share0, far)
    share2, share6 = swap(share0, "pop", 2), swap(share0, "pop", 6)
    part, pack = distance_parts(near, far, facts)
    part = part + swap(part, "dp", 1)
    pack = after(pack, part)
    part = part + swap(part, "dp", 2)
    pack = swap(pack, "dp", 12)
    part = part + swap(part, "dp", 4)
    dists = [part, swap(part, "dp", 8)]

    swapped0 = swap(after(share0, pack), "pop", 1)
    share0, share2, share4, share6 = after([share0, share2, share4, share6], pack, *dists)
    swapped = [swapped0] + [swap(v, "pop", 1) for v in (share2, share4, share6)]
    slope_a, turned_a = partner_part([share0, share2, share4, share6], w_hidden)
    dz, heads, marks, cents = coefficients(
        total_probes, dists, near, far, facts, pack, w_head, slope_a, slope, hid
    )
    dz_b, turned_b = partner_part(swapped, w_hidden, (marks, cents, pack))

    parts = [turned, turned_a, turned_b, dz, dz_b, heads]
    tie = lambda *first: parts[:3] + [after(dz, *first)] + parts[4:]
    early, last = range(len(CHUNKS) - 1), [len(CHUNKS) - 1]
    a2s, b2s = gradient(parts, [[0, 1], [2, 3]], early)
    from_a, from_b = [], []
    for i in early:
        from_a.append(shift_y(a2s[i], 1))
        from_b.append(shift_y(b2s[i], -1))
    away = [4 * g + k for g in range(4) for k in (2, 3)]
    waiting = []
    tied = tie(*a2s)
    for i in early:
        (ones,), (threes,), (zeros,) = gradient(tied, [[4, 5, 6, 7], [8, 9, 10, 11], [12, 13, 14, 15]], [i])
        if i == 0:
            ((sent,),) = gradient(tie(*a2s), [away], last)
            met = swap(sent, "dp", 4)
        ones, threes = add_into(ones, from_a[i], 0), add_into(threes, from_b[i], 2)
        waiting.append((zeros, shift_y(ones, 1), shift_y(threes, -1)))
        tied = tie(ones, threes)
    (a2,), (b2,), (ones,), (threes,), (zeros,) = gradient(tied, [[0], [1], [4, 5], [8, 9], [12, 13]], last, met)
    last_a, last_b = shift_y(a2, 1), shift_y(b2, -1)
    near_0, away_0 = fold(after(waiting[0], a2, b2), 2)
    met_0 = swap(away_0, "dp", 4)
    last_a, last_b = after((last_a, last_b), away_0)
    ones, threes = add_into(ones, last_a, 0), add_into(threes, last_b, 1)
    last_terms = (zeros, shift_y(ones, 1), shift_y(threes, -1))
    own_0, to_0 = fold((near_0, met_0), 1)
    other_0 = swap(to_0, "dp", 12)
    own_1, to_1 = fold(last_terms, 1)
    other_1 = swap(to_1, "dp", 12)
    pieces = [own_0, other_0, own_1, other_1]
    grad_one, grad_two = finish(pieces, w_head.shape[2] // 16)
    return grad_one, grad_two.transpose(1, 0, 2)


def solution(mesh):
    placed = (
        P("dp", None),
        P("dp"),
        P("dp"),
        P("pop", None, None),
        P("pop", None, None),
        P("pop", "dp"),
    )
    return jax.shard_map(
        body,
        mesh=mesh,
        in_specs=placed,
        out_specs=(P("pop", "dp", None), P("pop", None, "dp")),
        check_vma=False,
    )
```

profile of v0, /device:TPU:6, one launch (start us, length us, event | category | flops | bytes accessed | tf_op | source)
XLA Modules:
  0.0 123.7 jit_solution(4826246912411831794)
XLA Ops:
  2.1 5.9 %collective-permute-start = (f32[128,2048]{1,0:T(8,128)S(1)}, f32[128,2048]{1,0:T(8,128)S(1)}, u32[]{:S(2)}, u32[]{:S(2)}) collective-permute-start(f32[128,2048]{1,0:T(8,128)S(1)} %get-tuple-element.99), channel_id=1, source_target_pairs={{0,140},{1,141},{2,142},{3,143},{4,8},{5,9},{6,10},{7,11},{8,4},{9... | collective-permute-start | bytes 3145736 | tf_op jit(solution)/shard_map/ppermute | solution.py:498
  8.1 10.2 %forward.1 = (bf16[1024,1024]{1,0:T(8,128)(2,1)S(1)}, f32[1024,512]{1,0:T(8,128)S(1)}, bf16[16,128,1024]{2,1,0:T(8,128)(2,1)S(1)}, f32[1,1024]{1,0:T(1,128)S(1)}, f32[8,1024]{1,0:T(8,128)S(1)}) custom-call(bf16[1024,2048]{1,0:T(8,128)(2,1)} %pool_hbm.1, bf16[1,2048,1024]{2,1,0:T(8,128)(2,1)} %w_hbm.5, bf16[1,18,1024]{2,1,0:T(8,128)(2,1)S(1)} %copy-done.1, ...), custom_call_target="tpu_custom_call" | custom-call | flops 330000000 | tf_op jit(solution)/shard_map/forward/pallas_call | solution.py:138
  20.5 2.8 %collective-permute-done.2 = f32[2,1024]{1,0:T(2,128)S(1)} collective-permute-done((f32[2,1024]{1,0:T(2,128)S(1)}, f32[2,1024]{1,0:T(2,128)S(1)}, u32[]{:S(2)}, u32[]{:S(2)}) %collective-permute-start.2) | collective-permute-done | bytes 8224 | tf_op jit(solution)/shard_map/ppermute | solution.py:494
  24.9 3.8 %collective-permute-done.3 = f32[4,1024]{1,0:T(4,128)S(1)} collective-permute-done((f32[4,1024]{1,0:T(4,128)S(1)}, f32[4,1024]{1,0:T(4,128)S(1)}, u32[]{:S(2)}, u32[]{:S(2)}) %collective-permute-start.3) | collective-permute-done | bytes 16416 | tf_op jit(solution)/shard_map/ppermute | solution.py:494
  30.3 6.4 %collective-permute-done.4.far_ref = f32[8,1024]{1,0:T(8,128)S(1)} collective-permute-done((f32[8,1024]{1,0:T(8,128)S(1)}, f32[8,1024]{1,0:T(8,128)S(1)}, u32[]{:S(2)}, u32[]{:S(2)}) %collective-permute-start.4) | collective-permute-done | bytes 32800 | tf_op jit(solution)/shard_map/ppermute | solution.py:494
  40.9 2.1 %collective-permute-done.8 = f32[16,128]{1,0:T(8,128)S(1)} collective-permute-done((f32[16,128]{1,0:T(8,128)S(1)}, f32[16,128]{1,0:T(8,128)S(1)}, u32[]{:S(2)}, u32[]{:S(2)}) %collective-permute-start.8) | collective-permute-done | bytes 8224 | tf_op jit(solution)/shard_map/ppermute | solution.py:494
  43.0 1.8 %collective-permute-start.9 = (f32[24,1024]{1,0:T(8,128)S(1)}, f32[24,1024]{1,0:T(8,128)S(1)}, u32[]{:S(2)}, u32[]{:S(2)}) collective-permute-start(f32[24,1024]{1,0:T(8,128)S(1)} %get-tuple-element.57), channel_id=1, source_target_pairs={{0,12},{1,13},{2,14},{3,15},{4,8},{5,9},{6,10},{7,11},{8,4},{9,5},... | collective-permute-start | bytes 294920 | tf_op jit(solution)/shard_map/ppermute | solution.py:494
  44.7 3.2 %collective-permute-start.10 = (f32[16,128]{1,0:T(8,128)S(1)}, f32[16,128]{1,0:T(8,128)S(1)}, u32[]{:S(2)}, u32[]{:S(2)}) collective-permute-start(f32[16,128]{1,0:T(8,128)S(1)} %add.22), channel_id=1, source_target_pairs={{0,2},{1,3},{2,0},{3,1},{4,6},{5,7},{6,4},{7,5},{8,10},{9,11},{10,... | collective-permute-start | bytes 24584 | tf_op jit(solution)/shard_map/ppermute | solution.py:494
  48.0 1.9 %collective-permute-done.10 = f32[16,128]{1,0:T(8,128)S(1)} collective-permute-done((f32[16,128]{1,0:T(8,128)S(1)}, f32[16,128]{1,0:T(8,128)S(1)}, u32[]{:S(2)}, u32[]{:S(2)}) %collective-permute-start.10) | collective-permute-done | bytes 8224 | tf_op jit(solution)/shard_map/ppermute | solution.py:494
  49.9 3.6 %collective-permute-done.11 = f32[16,128]{1,0:T(8,128)S(1)} collective-permute-done((f32[16,128]{1,0:T(8,128)S(1)}, f32[16,128]{1,0:T(8,128)S(1)}, u32[]{:S(2)}, u32[]{:S(2)}) %collective-permute-start.11) | collective-permute-done | bytes 8224 | tf_op jit(solution)/shard_map/ppermute | solution.py:494
  54.2 7.2 %collective-permute-done.12.d1 = f32[16,128]{1,0:T(8,128)S(1)} collective-permute-done((f32[16,128]{1,0:T(8,128)S(1)}, f32[16,128]{1,0:T(8,128)S(1)}, u32[]{:S(2)}, u32[]{:S(2)}) %collective-permute-start.12) | collective-permute-done | bytes 8224 | tf_op jit(solution)/shard_map/ppermute | solution.py:494
  62.1 2.0 %partner.2 = (f32[512,512]{1,0:T(8,128)S(1)}, bf16[16,128,512]{2,1,0:T(8,128)(2,1)S(1)}) custom-call(f32[128,2048]{1,0:T(8,128)S(1)} %collective-permute-done.a_ref, f32[128,2048]{1,0:T(8,128)S(1)} %collective-permute-done.5.b_ref, f32[128,2048]{1,0:T(8,128)S(1)} %collective-permute-done.6.c_ref, f32[128,2048]{1,0:T(8,128)S(1)} %collective-permute-done.7.d_ref, ...), custom_call_target="tpu_custom_call" | custom-call | flops 330000000 | tf_op jit(solution)/shard_map/partner/pallas_call | solution.py:242
  64.1 5.0 %coefficients.1 = (bf16[1536,512]{1,0:T(8,128)(2,1)S(1)}, f32[16,8,512]{2,1,0:T(8,128)S(1)}, bf16[96,1024]{1,0:T(8,128)(2,1)S(1)}, bf16[96,512]{1,0:T(8,128)(2,1)S(1)}) custom-call(f32[16,128]{1,0:T(8,128)S(1)} %add.24.d0, f32[16,128]{1,0:T(8,128)S(1)} %collective-permute-done.12.d1, f32[8,1024]{1,0:T(8,128)S(1)} %pad_maximum_fusion.near_ref, ...), custom_call_target="tpu_custom_call" | custom-call | flops 330000000 | tf_op jit(solution)/shard_map/coefficients/pallas_call | solution.py:331
  69.1 3.0 %partner.3 = (bf16[512,512]{1,0:T(8,128)(2,1)S(1)}, bf16[16,128,512]{2,1,0:T(8,128)(2,1)S(1)}) custom-call(f32[128,2048]{1,0:T(8,128)S(1)} %collective-permute-done.13.a_ref, f32[128,2048]{1,0:T(8,128)S(1)} %collective-permute-done.14.b_ref, f32[128,2048]{1,0:T(8,128)S(1)} %collective-permute-done.15.c_ref, f32[128,2048]{1,0:T(8,128)S(1)} %collective-permute-done.16.d_ref, ...), custom_call_target="tpu_custom_call" | custom-call | flops 330000000 | tf_op jit(solution)/shard_map/partner/pallas_call | solution.py:242
  73.0 1.7 %collective-permute-start.17 = (f32[2,80,512]{2,1,0:T(8,128)S(1)}, f32[2,80,512]{2,1,0:T(8,128)S(1)}, u32[]{:S(2)}, u32[]{:S(2)}) collective-permute-start(f32[2,80,512]{2,1,0:T(8,128)S(1)} %get-tuple-element.73), channel_id=1, source_target_pairs={{0,1},{1,2},{2,3},{3,0},{4,5},{5,6},{6,7},{7,4},{8,9},{9,10},{10,1... | collective-permute-start | bytes 983048 | tf_op jit(solution)/shard_map/ppermute | solution.py:490
  79.0 2.3 %gradient.5 = (f32[4,80,512]{2,1,0:T(8,128)S(1)}, f32[4,80,512]{2,1,0:T(8,128)S(1)}, f32[4,80,512]{2,1,0:T(8,128)S(1)}) custom-call(bf16[16,128,1024]{2,1,0:T(8,128)(2,1)S(1)} %get-tuple-element.50.refs_0_, bf16[16,128,512]{2,1,0:T(8,128)(2,1)S(1)} %get-tuple-element.62.refs_1_, bf16[16,128,512]{2,1,0:T(8,128)(2,1)S(1)} %get-tuple-element.69.refs_2_, ...), custom_call_target="tpu_custom_call" | custom-call | flops 330000000 | tf_op jit(solution)/shard_map/gradient/pallas_call | solution.py:399
  81.2 3.1 %collective-permute-done.17.more_ref = f32[2,80,512]{2,1,0:T(8,128)S(1)} collective-permute-done((f32[2,80,512]{2,1,0:T(8,128)S(1)}, f32[2,80,512]{2,1,0:T(8,128)S(1)}, u32[]{:S(2)}, u32[]{:S(2)}) %collective-permute-start.17) | collective-permute-done | bytes 327712 | tf_op jit(solution)/shard_map/ppermute | solution.py:490
  84.9 3.0 %collective-permute-start.20 = (f32[4,80,512]{2,1,0:T(8,128)S(1)}, f32[4,80,512]{2,1,0:T(8,128)S(1)}, u32[]{:S(2)}, u32[]{:S(2)}) collective-permute-start(f32[4,80,512]{2,1,0:T(8,128)S(1)} %add_into.5), channel_id=1, source_target_pairs={{0,3},{1,0},{2,1},{3,2},{4,7},{5,4},{6,5},{7,6},{8,11},{9,8},{10,9... | collective-permute-start | bytes 1966088 | tf_op jit(solution)/shard_map/ppermute | solution.py:490
  87.9 12.5 %collective-permute-done.21.refs_6_ = f32[8,56,512]{2,1,0:T(8,128)S(1)} collective-permute-done((f32[8,56,512]{2,1,0:T(8,128)S(1)}, f32[8,56,512]{2,1,0:T(8,128)S(1)}, u32[]{:S(2)}, u32[]{:S(2)}) %collective-permute-start.21) | collective-permute-done | bytes 917536 | tf_op jit(solution)/shard_map/ppermute | solution.py:494
  102.9 2.9 %collective-permute-start.25 = (f32[1,56,512]{2,1,0:T(8,128)S(1)}, f32[1,56,512]{2,1,0:T(8,128)S(1)}, u32[]{:S(2)}, u32[]{:S(2)}) collective-permute-start(f32[1,56,512]{2,1,0:T(8,128)S(1)} %get-tuple-element.81), channel_id=1, source_target_pairs={{0,3},{1,0},{2,1},{3,2},{4,7},{5,4},{6,5},{7,6},{8,11},{9,8},{10,9... | collective-permute-start | bytes 344072 | tf_op jit(solution)/shard_map/ppermute | solution.py:490
  105.9 2.8 %collective-permute-done.24.more_ref = f32[1,56,512]{2,1,0:T(8,128)S(1)} collective-permute-done((f32[1,56,512]{2,1,0:T(8,128)S(1)}, f32[1,56,512]{2,1,0:T(8,128)S(1)}, u32[]{:S(2)}, u32[]{:S(2)}) %collective-permute-start.24) | collective-permute-done | bytes 114720 | tf_op jit(solution)/shard_map/ppermute | solution.py:490
  109.9 2.2 %collective-permute-start.27 = (f32[2,56,512]{2,1,0:T(8,128)S(1)}, f32[2,56,512]{2,1,0:T(8,128)S(1)}, u32[]{:S(2)}, u32[]{:S(2)}) collective-permute-start(f32[2,56,512]{2,1,0:T(8,128)S(1)} %add_into.7), channel_id=1, source_target_pairs={{0,3},{1,0},{2,1},{3,2},{4,7},{5,4},{6,5},{7,6},{8,11},{9,8},{10,9... | collective-permute-start | bytes 688136 | tf_op jit(solution)/shard_map/ppermute | solution.py:490
  113.6 2.3 %collective-permute-done.26.refs_1_ = f32[2,56,512]{2,1,0:T(8,128)S(1)} collective-permute-done((f32[2,56,512]{2,1,0:T(8,128)S(1)}, f32[2,56,512]{2,1,0:T(8,128)S(1)}, u32[]{:S(2)}, u32[]{:S(2)}) %collective-permute-start.26) | collective-permute-done | bytes 229408 | tf_op jit(solution)/shard_map/ppermute | solution.py:490
  117.5 5.3 %collective-permute-done.28.refs_3_ = f32[1,56,512]{2,1,0:T(8,128)S(1)} collective-permute-done((f32[1,56,512]{2,1,0:T(8,128)S(1)}, f32[1,56,512]{2,1,0:T(8,128)S(1)}, u32[]{:S(2)}, u32[]{:S(2)}) %collective-permute-start.28) | collective-permute-done | bytes 114720 | tf_op jit(solution)/shard_map/ppermute | solution.py:494
  (68 shorter events, 25.8 us)
Async XLA Ops:
  2.1 35.0 %collective-permute-start = (f32[128,2048]{1,0:T(8,128)S(1)}, f32[128,2048]{1,0:T(8,128)S(1)}, u32[]{:S(2)}, u32[]{:S(2)}) collective-permute-start(f32[128,2048]{1,0:T(8,128)S(1)} %get-tuple-element.99), channel_id=1, source_target_pairs={{0,140},{1,141},{2,142},{3,143},{4,8},{5,9},{6,10},{7,11},{8,4},{9... | collective-permute-start | bytes 3145736 | tf_op jit(solution)/shard_map/ppermute | solution.py:498
  23.4 5.3 %collective-permute-start.3 = (f32[4,1024]{1,0:T(4,128)S(1)}, f32[4,1024]{1,0:T(4,128)S(1)}, u32[]{:S(2)}, u32[]{:S(2)}) collective-permute-start(f32[4,1024]{1,0:T(4,128)S(1)} %pad_maximum_fusion.1), channel_id=1, source_target_pairs={{0,64},{16,80},{32,96},{48,112},{64,0},{80,16},{96,32},{112,48},{1... | collective-permute-start | bytes 49160 | tf_op jit(solution)/shard_map/ppermute | solution.py:494
  28.7 7.9 %collective-permute-start.4 = (f32[8,1024]{1,0:T(8,128)S(1)}, f32[8,1024]{1,0:T(8,128)S(1)}, u32[]{:S(2)}, u32[]{:S(2)}) collective-permute-start(f32[8,1024]{1,0:T(8,128)S(1)} %pad_maximum_fusion.near_ref), channel_id=1, source_target_pairs={{0,128},{16,144},{32,160},{48,176},{64,192},{80,208},{96,224},{112... | collective-permute-start | bytes 98312 | tf_op jit(solution)/shard_map/ppermute | solution.py:494
  36.6 24.8 %collective-permute-start.6 = (f32[128,2048]{1,0:T(8,128)S(1)}, f32[128,2048]{1,0:T(8,128)S(1)}, u32[]{:S(2)}, u32[]{:S(2)}) collective-permute-start(f32[128,2048]{1,0:T(8,128)S(1)} %get-tuple-element.53), channel_id=1, source_target_pairs={{0,140},{1,141},{2,142},{3,143},{4,8},{5,9},{6,10},{7,11},{8,4},{9... | collective-permute-start | bytes 3145736 | tf_op jit(solution)/shard_map/ppermute | solution.py:498
  37.1 24.3 %collective-permute-start.5 = (f32[128,2048]{1,0:T(8,128)S(1)}, f32[128,2048]{1,0:T(8,128)S(1)}, u32[]{:S(2)}, u32[]{:S(2)}) collective-permute-start(f32[128,2048]{1,0:T(8,128)S(1)} %collective-permute-done.a_ref), channel_id=1, source_target_pairs={{0,32},{16,48},{32,0},{48,16},{64,96},{80,112},{96,64},{112,80},{1... | collective-permute-start | bytes 3145736 | tf_op jit(solution)/shard_map/ppermute | solution.py:494
  37.9 23.5 %collective-permute-start.7 = (f32[128,2048]{1,0:T(8,128)S(1)}, f32[128,2048]{1,0:T(8,128)S(1)}, u32[]{:S(2)}, u32[]{:S(2)}) collective-permute-start(f32[128,2048]{1,0:T(8,128)S(1)} %collective-permute-done.a_ref), channel_id=1, source_target_pairs={{0,96},{16,112},{32,64},{48,80},{64,32},{80,48},{96,0},{112,16},{1... | collective-permute-start | bytes 3145736 | tf_op jit(solution)/shard_map/ppermute | solution.py:494
  43.0 11.2 %collective-permute-start.9 = (f32[24,1024]{1,0:T(8,128)S(1)}, f32[24,1024]{1,0:T(8,128)S(1)}, u32[]{:S(2)}, u32[]{:S(2)}) collective-permute-start(f32[24,1024]{1,0:T(8,128)S(1)} %get-tuple-element.57), channel_id=1, source_target_pairs={{0,12},{1,13},{2,14},{3,15},{4,8},{5,9},{6,10},{7,11},{8,4},{9,5},... | collective-permute-start | bytes 294920 | tf_op jit(solution)/shard_map/ppermute | solution.py:494
  53.6 7.8 %collective-permute-start.12 = (f32[16,128]{1,0:T(8,128)S(1)}, f32[16,128]{1,0:T(8,128)S(1)}, u32[]{:S(2)}, u32[]{:S(2)}) collective-permute-start(f32[16,128]{1,0:T(8,128)S(1)} %add.24.d0), channel_id=1, source_target_pairs={{0,8},{1,9},{2,10},{3,11},{4,12},{5,13},{6,14},{7,15},{8,0},{9,1},... | collective-permute-start | bytes 24584 | tf_op jit(solution)/shard_map/ppermute | solution.py:494
  54.2 14.9 %collective-permute-start.13 = (f32[128,2048]{1,0:T(8,128)S(1)}, f32[128,2048]{1,0:T(8,128)S(1)}, u32[]{:S(2)}, u32[]{:S(2)}) collective-permute-start(f32[128,2048]{1,0:T(8,128)S(1)} %collective-permute-done.a_ref), channel_id=1, source_target_pairs={{0,16},{16,0},{32,48},{48,32},{64,80},{80,64},{96,112},{112,96},{1... | collective-permute-start | bytes 3145736 | tf_op jit(solution)/shard_map/ppermute | solution.py:494
  61.4 7.6 %collective-permute-start.14 = (f32[128,2048]{1,0:T(8,128)S(1)}, f32[128,2048]{1,0:T(8,128)S(1)}, u32[]{:S(2)}, u32[]{:S(2)}) collective-permute-start(f32[128,2048]{1,0:T(8,128)S(1)} %collective-permute-done.5.b_ref), channel_id=1, source_target_pairs={{0,16},{16,0},{32,48},{48,32},{64,80},{80,64},{96,112},{112,96},{1... | collective-permute-start | bytes 3145736 | tf_op jit(solution)/shard_map/ppermute | solution.py:494
  61.5 7.6 %collective-permute-start.15 = (f32[128,2048]{1,0:T(8,128)S(1)}, f32[128,2048]{1,0:T(8,128)S(1)}, u32[]{:S(2)}, u32[]{:S(2)}) collective-permute-start(f32[128,2048]{1,0:T(8,128)S(1)} %collective-permute-done.6.c_ref), channel_id=1, source_target_pairs={{0,16},{16,0},{32,48},{48,32},{64,80},{80,64},{96,112},{112,96},{1... | collective-permute-start | bytes 3145736 | tf_op jit(solution)/shard_map/ppermute | solution.py:494
  62.0 7.1 %collective-permute-start.16 = (f32[128,2048]{1,0:T(8,128)S(1)}, f32[128,2048]{1,0:T(8,128)S(1)}, u32[]{:S(2)}, u32[]{:S(2)}) collective-permute-start(f32[128,2048]{1,0:T(8,128)S(1)} %collective-permute-done.7.d_ref), channel_id=1, source_target_pairs={{0,16},{16,0},{32,48},{48,32},{64,80},{80,64},{96,112},{112,96},{1... | collective-permute-start | bytes 3145736 | tf_op jit(solution)/shard_map/ppermute | solution.py:494
  73.0 11.4 %collective-permute-start.17 = (f32[2,80,512]{2,1,0:T(8,128)S(1)}, f32[2,80,512]{2,1,0:T(8,128)S(1)}, u32[]{:S(2)}, u32[]{:S(2)}) collective-permute-start(f32[2,80,512]{2,1,0:T(8,128)S(1)} %get-tuple-element.73), channel_id=1, source_target_pairs={{0,1},{1,2},{2,3},{3,0},{4,5},{5,6},{6,7},{7,4},{8,9},{9,10},{10,1... | collective-permute-start | bytes 983048 | tf_op jit(solution)/shard_map/ppermute | solution.py:490
  74.6 10.2 %collective-permute-start.19 = (f32[2,80,512]{2,1,0:T(8,128)S(1)}, f32[2,80,512]{2,1,0:T(8,128)S(1)}, u32[]{:S(2)}, u32[]{:S(2)}) collective-permute-start(f32[2,80,512]{2,1,0:T(8,128)S(1)} %get-tuple-element.78), channel_id=1, source_target_pairs={{0,3},{1,0},{2,1},{3,2},{4,7},{5,4},{6,5},{7,6},{8,11},{9,8},{10,9... | collective-permute-start | bytes 983048 | tf_op jit(solution)/shard_map/ppermute | solution.py:490
  77.8 22.6 %collective-permute-start.21 = (f32[8,56,512]{2,1,0:T(8,128)S(1)}, f32[8,56,512]{2,1,0:T(8,128)S(1)}, u32[]{:S(2)}, u32[]{:S(2)}) collective-permute-start(f32[8,56,512]{2,1,0:T(8,128)S(1)} %gradient.6), channel_id=1, source_target_pairs={{0,4},{1,5},{2,6},{3,7},{4,0},{5,1},{6,2},{7,3},{8,12},{9,13},{10,... | collective-permute-start | bytes 2752520 | tf_op jit(solution)/shard_map/ppermute | solution.py:494
  84.4 17.6 %collective-permute-start.18 = (f32[4,80,512]{2,1,0:T(8,128)S(1)}, f32[4,80,512]{2,1,0:T(8,128)S(1)}, u32[]{:S(2)}, u32[]{:S(2)}) collective-permute-start(f32[4,80,512]{2,1,0:T(8,128)S(1)} %add_into.4), channel_id=1, source_target_pairs={{0,1},{1,2},{2,3},{3,0},{4,5},{5,6},{6,7},{7,4},{8,9},{9,10},{10,1... | collective-permute-start | bytes 1966088 | tf_op jit(solution)/shard_map/ppermute | solution.py:490
  84.9 17.2 %collective-permute-start.20 = (f32[4,80,512]{2,1,0:T(8,128)S(1)}, f32[4,80,512]{2,1,0:T(8,128)S(1)}, u32[]{:S(2)}, u32[]{:S(2)}) collective-permute-start(f32[4,80,512]{2,1,0:T(8,128)S(1)} %add_into.5), channel_id=1, source_target_pairs={{0,3},{1,0},{2,1},{3,2},{4,7},{5,4},{6,5},{7,6},{8,11},{9,8},{10,9... | collective-permute-start | bytes 1966088 | tf_op jit(solution)/shard_map/ppermute | solution.py:490
  102.1 10.0 %collective-permute-start.22 = (f32[2,80,512]{2,1,0:T(8,128)S(1)}, f32[2,80,512]{2,1,0:T(8,128)S(1)}, u32[]{:S(2)}, u32[]{:S(2)}) collective-permute-start(f32[2,80,512]{2,1,0:T(8,128)S(1)} %get-tuple-element.86), channel_id=1, source_target_pairs={{0,4},{1,5},{2,6},{3,7},{4,0},{5,1},{6,2},{7,3},{8,12},{9,13},{10,... | collective-permute-start | bytes 983048 | tf_op jit(solution)/shard_map/ppermute | solution.py:494
  102.6 6.0 %collective-permute-start.24 = (f32[1,56,512]{2,1,0:T(8,128)S(1)}, f32[1,56,512]{2,1,0:T(8,128)S(1)}, u32[]{:S(2)}, u32[]{:S(2)}) collective-permute-start(f32[1,56,512]{2,1,0:T(8,128)S(1)} %get-tuple-element.80), channel_id=1, source_target_pairs={{0,1},{1,2},{2,3},{3,0},{4,5},{5,6},{6,7},{7,4},{8,9},{9,10},{10,1... | collective-permute-start | bytes 344072 | tf_op jit(solution)/shard_map/ppermute | solution.py:490
  102.9 5.7 %collective-permute-start.25 = (f32[1,56,512]{2,1,0:T(8,128)S(1)}, f32[1,56,512]{2,1,0:T(8,128)S(1)}, u32[]{:S(2)}, u32[]{:S(2)}) collective-permute-start(f32[1,56,512]{2,1,0:T(8,128)S(1)} %get-tuple-element.81), channel_id=1, source_target_pairs={{0,3},{1,0},{2,1},{3,2},{4,7},{5,4},{6,5},{7,6},{8,11},{9,8},{10,9... | collective-permute-start | bytes 344072 | tf_op jit(solution)/shard_map/ppermute | solution.py:490
  108.7 7.3 %collective-permute-start.26 = (f32[2,56,512]{2,1,0:T(8,128)S(1)}, f32[2,56,512]{2,1,0:T(8,128)S(1)}, u32[]{:S(2)}, u32[]{:S(2)}) collective-permute-start(f32[2,56,512]{2,1,0:T(8,128)S(1)} %add_into.6), channel_id=1, source_target_pairs={{0,1},{1,2},{2,3},{3,0},{4,5},{5,6},{6,7},{7,4},{8,9},{9,10},{10,1... | collective-permute-start | bytes 688136 | tf_op jit(solution)/shard_map/ppermute | solution.py:490
  109.9 6.1 %collective-permute-start.27 = (f32[2,56,512]{2,1,0:T(8,128)S(1)}, f32[2,56,512]{2,1,0:T(8,128)S(1)}, u32[]{:S(2)}, u32[]{:S(2)}) collective-permute-start(f32[2,56,512]{2,1,0:T(8,128)S(1)} %add_into.7), channel_id=1, source_target_pairs={{0,3},{1,0},{2,1},{3,2},{4,7},{5,4},{6,5},{7,6},{8,11},{9,8},{10,9... | collective-permute-start | bytes 688136 | tf_op jit(solution)/shard_map/ppermute | solution.py:490
  112.1 10.7 %collective-permute-start.23 = (f32[1,80,512]{2,1,0:T(8,128)S(1)}, f32[1,80,512]{2,1,0:T(8,128)S(1)}, u32[]{:S(2)}, u32[]{:S(2)}) collective-permute-start(f32[1,80,512]{2,1,0:T(8,128)S(1)} %get-tuple-element.88), channel_id=1, source_target_pairs={{0,12},{1,13},{2,14},{3,15},{4,8},{5,9},{6,10},{7,11},{8,4},{9,5},... | collective-permute-start | bytes 491528 | tf_op jit(solution)/shard_map/ppermute | solution.py:494
  116.0 6.8 %collective-permute-start.28 = (f32[1,56,512]{2,1,0:T(8,128)S(1)}, f32[1,56,512]{2,1,0:T(8,128)S(1)}, u32[]{:S(2)}, u32[]{:S(2)}) collective-permute-start(f32[1,56,512]{2,1,0:T(8,128)S(1)} %get-tuple-element.95), channel_id=1, source_target_pairs={{0,12},{1,13},{2,14},{3,15},{4,8},{5,9},{6,10},{7,11},{8,4},{9,5},... | collective-permute-start | bytes 344072 | tf_op jit(solution)/shard_map/ppermute | solution.py:494
  (10 other events, 101.3 us)
where the time goes:
time: 124 us
  waiting for transfers between devices  55.3 us (45%)
  starting transfers between devices  38.4 us (31%)
  Pallas kernels  27.6 us (22%)
  other arithmetic  1.5 us (1%)
    ppermute x19, waiting for transfers between devices, swap(): return lax.ppermute(v, axis, [(i, i ^ mask) for i in range(16)])  46.8 us
    ppermute x19, starting transfers between devices, swap(): return lax.ppermute(v, axis, [(i, i ^ mask) for i in range(16)])  18.6 us
    ppermute x8, starting transfers between devices, shift_y(): lax.ppermute(v, 'dp', [(z * 4 + y, z * 4 + (y + s) % 4) for z in range(4)...  13.3 us
    pallas_call x1, Pallas kernels, forward(): pl.pallas_call(forward_kernel, in_specs=[HBM_SPEC] * 2 + [VMEM_SPEC] * 4,...  10.2 us
    ppermute x8, waiting for transfers between devices, shift_y(): lax.ppermute(v, 'dp', [(z * 4 + y, z * 4 + (y + s) % 4) for z in range(4)...  8.43 us
    ppermute x2, starting transfers between devices, to_partner_rows(): lax.ppermute(v, ('pop', 'dp'), [(p * 16 + d, (p ^ (8 if d // 4 in (0, 3)...  6.4 us
    pallas_call x4, Pallas kernels, gradient(): pl.pallas_call(functools.partial(grad_kernel, plan), in_specs=[VMEM_SPEC]...  6.12 us
    pallas_call x1, Pallas kernels, coefficients(): pl.pallas_call(functools.partial(coeff_kernel, total_probes, scaling), in...  4.97 us
  transfers between devices with their start and end apart: 29, of which 14 were waited for; matrix products, arithmetic and copies ran while one was open for 0% of the time, Pallas kernels for 18%

commit v1 on v0

--- a/solution.py
+++ b/solution.py
@@ -377,7 +377,7 @@
 def gradient(parts, groups, which, more=None):
     dz = parts[3]
     width = dz.shape[1]
-    chunks = [(sum(CHUNKS[:c]), CHUNKS[c], c == len(CHUNKS) - 1) for c in which]
+    chunks = [(sum(CHUNKS[:c]), CHUNKS[c], c == 0) for c in which]
     begin, end = chunks[0][0], chunks[-1][0] + chunks[-1][1]
     shapes = [
         jax.ShapeDtypeStruct((len(group), size + (EXTRA if extra else 0), width), F32)
@@ -459,7 +459,7 @@
         out_ref[0, at : at + size, left] = own[0, 0:size, :]
         out_ref[0, at : at + size, right] = other[0, 0:size, :]
         at += size
-    heads = own[0, CHUNKS[-1] :, :] + other[0, CHUNKS[-1] :, :]
+    heads = refs[0][0, CHUNKS[0] :, :] + refs[1][0, CHUNKS[0] :, :]
     cols = two_ref.shape[2]
     for g in range(3):
         count = min(EXTRA, ACTIONS - g * EXTRA)

time: 124 us -> 126 us (1.016)
  waiting for transfers between devices: 55.3 us -> 56.8 us
    ppermute x8, waiting for transfers between devices: 8.43 us -> 13.7 us  [shift_y(): lax.ppermute(v, 'dp', [(z * 4 + y, z * 4 + (y + s) % 4) for z in range(4)...]
    ppermute x19, waiting for transfers between devices: 46.8 us -> 43.1 us  [swap(): return lax.ppermute(v, axis, [(i, i ^ mask) for i in range(16)])]
  transfers between devices with their start and end apart: 29 -> 29, of which waited for: 14 -> 15; matrix products, arithmetic and copies ran while one was open for 0% -> 0% of each run, Pallas kernels for 18% -> 18%
where the time goes in v1:
time: 126 us; the launch traced here: 125 us
  waiting for transfers between devices  56.8 us (45%)
  starting transfers between devices  38.2 us (30%)
  Pallas kernels  27.6 us (22%)
  other arithmetic  1.5 us (1%)
    ppermute x19, waiting for transfers between devices, swap(): return lax.ppermute(v, axis, [(i, i ^ mask) for i in range(16)])  43.1 us
    ppermute x19, starting transfers between devices, swap(): return lax.ppermute(v, axis, [(i, i ^ mask) for i in range(16)])  18.5 us
    ppermute x8, waiting for transfers between devices, shift_y(): lax.ppermute(v, 'dp', [(z * 4 + y, z * 4 + (y + s) % 4) for z in range(4)...  13.7 us
    ppermute x8, starting transfers between devices, shift_y(): lax.ppermute(v, 'dp', [(z * 4 + y, z * 4 + (y + s) % 4) for z in range(4)...  13.3 us
    pallas_call x1, Pallas kernels, forward(): pl.pallas_call(forward_kernel, in_specs=[HBM_SPEC] * 2 + [VMEM_SPEC] * 4,...  10.2 us
    ppermute x2, starting transfers between devices, to_partner_rows(): lax.ppermute(v, ('pop', 'dp'), [(p * 16 + d, (p ^ (8 if d // 4 in (0, 3)...  6.4 us
    pallas_call x4, Pallas kernels, gradient(): pl.pallas_call(functools.partial(grad_kernel, plan), in_specs=[VMEM_SPEC]...  6.11 us
    pallas_call x1, Pallas kernels, coefficients(): pl.pallas_call(functools.partial(coeff_kernel, total_probes, scaling), in...  4.97 us
  transfers between devices with their start and end apart: 29, of which 15 were waited for; matrix products, arithmetic and copies ran while one was open for 0% of the time, Pallas kernels for 18%

profile of v1, /device:TPU:6, one launch (start us, length us, event | category | flops | bytes accessed | tf_op | source)
XLA Modules:
  0.0 125.1 jit_solution(3924671804552133879)
XLA Ops:
  2.1 5.9 %collective-permute-start = (f32[128,2048]{1,0:T(8,128)S(1)}, f32[128,2048]{1,0:T(8,128)S(1)}, u32[]{:S(2)}, u32[]{:S(2)}) collective-permute-start(f32[128,2048]{1,0:T(8,128)S(1)} %get-tuple-element.99), channel_id=1, source_target_pairs={{0,140},{1,141},{2,142},{3,143},{4,8},{5,9},{6,10},{7,11},{8,4},{9... | collective-permute-start | bytes 3145736 | tf_op jit(solution)/shard_map/ppermute | solution.py:498
  8.1 10.2 %forward.1 = (bf16[1024,1024]{1,0:T(8,128)(2,1)S(1)}, f32[1024,512]{1,0:T(8,128)S(1)}, bf16[16,128,1024]{2,1,0:T(8,128)(2,1)S(1)}, f32[1,1024]{1,0:T(1,128)S(1)}, f32[8,1024]{1,0:T(8,128)S(1)}) custom-call(bf16[1024,2048]{1,0:T(8,128)(2,1)} %pool_hbm.1, bf16[1,2048,1024]{2,1,0:T(8,128)(2,1)} %w_hbm.5, bf16[1,18,1024]{2,1,0:T(8,128)(2,1)S(1)} %copy-done.1, ...), custom_call_target="tpu_custom_call" | custom-call | flops 330000000 | tf_op jit(solution)/shard_map/forward/pallas_call | solution.py:138
  20.5 2.8 %collective-permute-done.2 = f32[2,1024]{1,0:T(2,128)S(1)} collective-permute-done((f32[2,1024]{1,0:T(2,128)S(1)}, f32[2,1024]{1,0:T(2,128)S(1)}, u32[]{:S(2)}, u32[]{:S(2)}) %collective-permute-start.2) | collective-permute-done | bytes 8224 | tf_op jit(solution)/shard_map/ppermute | solution.py:494
  24.9 3.8 %collective-permute-done.3 = f32[4,1024]{1,0:T(4,128)S(1)} collective-permute-done((f32[4,1024]{1,0:T(4,128)S(1)}, f32[4,1024]{1,0:T(4,128)S(1)}, u32[]{:S(2)}, u32[]{:S(2)}) %collective-permute-start.3) | collective-permute-done | bytes 16416 | tf_op jit(solution)/shard_map/ppermute | solution.py:494
  30.3 6.4 %collective-permute-done.4.far_ref = f32[8,1024]{1,0:T(8,128)S(1)} collective-permute-done((f32[8,1024]{1,0:T(8,128)S(1)}, f32[8,1024]{1,0:T(8,128)S(1)}, u32[]{:S(2)}, u32[]{:S(2)}) %collective-permute-start.4) | collective-permute-done | bytes 32800 | tf_op jit(solution)/shard_map/ppermute | solution.py:494
  40.9 2.1 %collective-permute-done.8 = f32[16,128]{1,0:T(8,128)S(1)} collective-permute-done((f32[16,128]{1,0:T(8,128)S(1)}, f32[16,128]{1,0:T(8,128)S(1)}, u32[]{:S(2)}, u32[]{:S(2)}) %collective-permute-start.8) | collective-permute-done | bytes 8224 | tf_op jit(solution)/shard_map/ppermute | solution.py:494
  43.0 1.8 %collective-permute-start.9 = (f32[24,1024]{1,0:T(8,128)S(1)}, f32[24,1024]{1,0:T(8,128)S(1)}, u32[]{:S(2)}, u32[]{:S(2)}) collective-permute-start(f32[24,1024]{1,0:T(8,128)S(1)} %get-tuple-element.57), channel_id=1, source_target_pairs={{0,12},{1,13},{2,14},{3,15},{4,8},{5,9},{6,10},{7,11},{8,4},{9,5},... | collective-permute-start | bytes 294920 | tf_op jit(solution)/shard_map/ppermute | solution.py:494
  44.7 3.2 %collective-permute-start.10 = (f32[16,128]{1,0:T(8,128)S(1)}, f32[16,128]{1,0:T(8,128)S(1)}, u32[]{:S(2)}, u32[]{:S(2)}) collective-permute-start(f32[16,128]{1,0:T(8,128)S(1)} %add.22), channel_id=1, source_target_pairs={{0,2},{1,3},{2,0},{3,1},{4,6},{5,7},{6,4},{7,5},{8,10},{9,11},{10,... | collective-permute-start | bytes 24584 | tf_op jit(solution)/shard_map/ppermute | solution.py:494
  48.0 1.9 %collective-permute-done.10 = f32[16,128]{1,0:T(8,128)S(1)} collective-permute-done((f32[16,128]{1,0:T(8,128)S(1)}, f32[16,128]{1,0:T(8,128)S(1)}, u32[]{:S(2)}, u32[]{:S(2)}) %collective-permute-start.10) | collective-permute-done | bytes 8224 | tf_op jit(solution)/shard_map/ppermute | solution.py:494
  49.9 3.6 %collective-permute-done.11 = f32[16,128]{1,0:T(8,128)S(1)} collective-permute-done((f32[16,128]{1,0:T(8,128)S(1)}, f32[16,128]{1,0:T(8,128)S(1)}, u32[]{:S(2)}, u32[]{:S(2)}) %collective-permute-start.11) | collective-permute-done | bytes 8224 | tf_op jit(solution)/shard_map/ppermute | solution.py:494
  54.2 7.2 %collective-permute-done.12.d1 = f32[16,128]{1,0:T(8,128)S(1)} collective-permute-done((f32[16,128]{1,0:T(8,128)S(1)}, f32[16,128]{1,0:T(8,128)S(1)}, u32[]{:S(2)}, u32[]{:S(2)}) %collective-permute-start.12) | collective-permute-done | bytes 8224 | tf_op jit(solution)/shard_map/ppermute | solution.py:494
  62.1 2.0 %partner.2 = (f32[512,512]{1,0:T(8,128)S(1)}, bf16[16,128,512]{2,1,0:T(8,128)(2,1)S(1)}) custom-call(f32[128,2048]{1,0:T(8,128)S(1)} %collective-permute-done.a_ref, f32[128,2048]{1,0:T(8,128)S(1)} %collective-permute-done.5.b_ref, f32[128,2048]{1,0:T(8,128)S(1)} %collective-permute-done.6.c_ref, f32[128,2048]{1,0:T(8,128)S(1)} %collective-permute-done.7.d_ref, ...), custom_call_target="tpu_custom_call" | custom-call | flops 330000000 | tf_op jit(solution)/shard_map/partner/pallas_call | solution.py:242
  64.1 5.0 %coefficients.1 = (bf16[1536,512]{1,0:T(8,128)(2,1)S(1)}, f32[16,8,512]{2,1,0:T(8,128)S(1)}, bf16[96,1024]{1,0:T(8,128)(2,1)S(1)}, bf16[96,512]{1,0:T(8,128)(2,1)S(1)}) custom-call(f32[16,128]{1,0:T(8,128)S(1)} %add.24.d0, f32[16,128]{1,0:T(8,128)S(1)} %collective-permute-done.12.d1, f32[8,1024]{1,0:T(8,128)S(1)} %pad_maximum_fusion.near_ref, ...), custom_call_target="tpu_custom_call" | custom-call | flops 330000000 | tf_op jit(solution)/shard_map/coefficients/pallas_call | solution.py:331
  69.1 3.0 %partner.3 = (bf16[512,512]{1,0:T(8,128)(2,1)S(1)}, bf16[16,128,512]{2,1,0:T(8,128)(2,1)S(1)}) custom-call(f32[128,2048]{1,0:T(8,128)S(1)} %collective-permute-done.13.a_ref, f32[128,2048]{1,0:T(8,128)S(1)} %collective-permute-done.14.b_ref, f32[128,2048]{1,0:T(8,128)S(1)} %collective-permute-done.15.c_ref, f32[128,2048]{1,0:T(8,128)S(1)} %collective-permute-done.16.d_ref, ...), custom_call_target="tpu_custom_call" | custom-call | flops 330000000 | tf_op jit(solution)/shard_map/partner/pallas_call | solution.py:242
  78.9 2.3 %gradient.5 = (f32[4,88,512]{2,1,0:T(8,128)S(1)}, f32[4,88,512]{2,1,0:T(8,128)S(1)}, f32[4,88,512]{2,1,0:T(8,128)S(1)}) custom-call(bf16[16,128,1024]{2,1,0:T(8,128)(2,1)S(1)} %get-tuple-element.50.refs_0_, bf16[16,128,512]{2,1,0:T(8,128)(2,1)S(1)} %get-tuple-element.62.refs_1_, bf16[16,128,512]{2,1,0:T(8,128)(2,1)S(1)} %get-tuple-element.69.refs_2_, ...), custom_call_target="tpu_custom_call" | custom-call | flops 330000000 | tf_op jit(solution)/shard_map/gradient/pallas_call | solution.py:399
  81.2 3.8 %collective-permute-done.17.more_ref = f32[2,88,512]{2,1,0:T(8,128)S(1)} collective-permute-done((f32[2,88,512]{2,1,0:T(8,128)S(1)}, f32[2,88,512]{2,1,0:T(8,128)S(1)}, u32[]{:S(2)}, u32[]{:S(2)}) %collective-permute-start.17) | collective-permute-done | bytes 360480 | tf_op jit(solution)/shard_map/ppermute | solution.py:490
  85.6 3.0 %collective-permute-start.20 = (f32[4,88,512]{2,1,0:T(8,128)S(1)}, f32[4,88,512]{2,1,0:T(8,128)S(1)}, u32[]{:S(2)}, u32[]{:S(2)}) collective-permute-start(f32[4,88,512]{2,1,0:T(8,128)S(1)} %add_into.5), channel_id=1, source_target_pairs={{0,3},{1,0},{2,1},{3,2},{4,7},{5,4},{6,5},{7,6},{8,11},{9,8},{10,9... | collective-permute-start | bytes 2162696 | tf_op jit(solution)/shard_map/ppermute | solution.py:490
  88.6 8.9 %collective-permute-done.21.refs_6_ = f32[8,48,512]{2,1,0:T(8,128)S(1)} collective-permute-done((f32[8,48,512]{2,1,0:T(8,128)S(1)}, f32[8,48,512]{2,1,0:T(8,128)S(1)}, u32[]{:S(2)}, u32[]{:S(2)}) %collective-permute-start.21) | collective-permute-done | bytes 786464 | tf_op jit(solution)/shard_map/ppermute | solution.py:494
  99.0 5.1 %collective-permute-done.18.refs_1_ = f32[4,88,512]{2,1,0:T(8,128)S(1)} collective-permute-done((f32[4,88,512]{2,1,0:T(8,128)S(1)}, f32[4,88,512]{2,1,0:T(8,128)S(1)}, u32[]{:S(2)}, u32[]{:S(2)}) %collective-permute-start.18) | collective-permute-done | bytes 720928 | tf_op jit(solution)/shard_map/ppermute | solution.py:490
  105.1 2.8 %collective-permute-start.25 = (f32[1,48,512]{2,1,0:T(8,128)S(1)}, f32[1,48,512]{2,1,0:T(8,128)S(1)}, u32[]{:S(2)}, u32[]{:S(2)}) collective-permute-start(f32[1,48,512]{2,1,0:T(8,128)S(1)} %get-tuple-element.81), channel_id=1, source_target_pairs={{0,3},{1,0},{2,1},{3,2},{4,7},{5,4},{6,5},{7,6},{8,11},{9,8},{10,9... | collective-permute-start | bytes 294920 | tf_op jit(solution)/shard_map/ppermute | solution.py:490
  107.8 2.6 %collective-permute-done.24.more_ref = f32[1,48,512]{2,1,0:T(8,128)S(1)} collective-permute-done((f32[1,48,512]{2,1,0:T(8,128)S(1)}, f32[1,48,512]{2,1,0:T(8,128)S(1)}, u32[]{:S(2)}, u32[]{:S(2)}) %collective-permute-start.24) | collective-permute-done | bytes 98336 | tf_op jit(solution)/shard_map/ppermute | solution.py:490
  111.8 2.0 %collective-permute-start.27 = (f32[2,48,512]{2,1,0:T(8,128)S(1)}, f32[2,48,512]{2,1,0:T(8,128)S(1)}, u32[]{:S(2)}, u32[]{:S(2)}) collective-permute-start(f32[2,48,512]{2,1,0:T(8,128)S(1)} %add_into.7), channel_id=1, source_target_pairs={{0,3},{1,0},{2,1},{3,2},{4,7},{5,4},{6,5},{7,6},{8,11},{9,8},{10,9... | collective-permute-start | bytes 589832 | tf_op jit(solution)/shard_map/ppermute | solution.py:490
  115.4 2.0 %collective-permute-done.26.refs_1_ = f32[2,48,512]{2,1,0:T(8,128)S(1)} collective-permute-done((f32[2,48,512]{2,1,0:T(8,128)S(1)}, f32[2,48,512]{2,1,0:T(8,128)S(1)}, u32[]{:S(2)}, u32[]{:S(2)}) %collective-permute-start.26) | collective-permute-done | bytes 196640 | tf_op jit(solution)/shard_map/ppermute | solution.py:490
  119.1 5.1 %collective-permute-done.28.refs_3_ = f32[1,48,512]{2,1,0:T(8,128)S(1)} collective-permute-done((f32[1,48,512]{2,1,0:T(8,128)S(1)}, f32[1,48,512]{2,1,0:T(8,128)S(1)}, u32[]{:S(2)}, u32[]{:S(2)}) %collective-permute-start.28) | collective-permute-done | bytes 98336 | tf_op jit(solution)/shard_map/ppermute | solution.py:494
  (68 shorter events, 27.6 us)
Async XLA Ops:
  2.1 35.0 %collective-permute-start = (f32[128,2048]{1,0:T(8,128)S(1)}, f32[128,2048]{1,0:T(8,128)S(1)}, u32[]{:S(2)}, u32[]{:S(2)}) collective-permute-start(f32[128,2048]{1,0:T(8,128)S(1)} %get-tuple-element.99), channel_id=1, source_target_pairs={{0,140},{1,141},{2,142},{3,143},{4,8},{5,9},{6,10},{7,11},{8,4},{9... | collective-permute-start | bytes 3145736 | tf_op jit(solution)/shard_map/ppermute | solution.py:498
  23.4 5.3 %collective-permute-start.3 = (f32[4,1024]{1,0:T(4,128)S(1)}, f32[4,1024]{1,0:T(4,128)S(1)}, u32[]{:S(2)}, u32[]{:S(2)}) collective-permute-start(f32[4,1024]{1,0:T(4,128)S(1)} %pad_maximum_fusion.1), channel_id=1, source_target_pairs={{0,64},{16,80},{32,96},{48,112},{64,0},{80,16},{96,32},{112,48},{1... | collective-permute-start | bytes 49160 | tf_op jit(solution)/shard_map/ppermute | solution.py:494
  28.7 7.9 %collective-permute-start.4 = (f32[8,1024]{1,0:T(8,128)S(1)}, f32[8,1024]{1,0:T(8,128)S(1)}, u32[]{:S(2)}, u32[]{:S(2)}) collective-permute-start(f32[8,1024]{1,0:T(8,128)S(1)} %pad_maximum_fusion.near_ref), channel_id=1, source_target_pairs={{0,128},{16,144},{32,160},{48,176},{64,192},{80,208},{96,224},{112... | collective-permute-start | bytes 98312 | tf_op jit(solution)/shard_map/ppermute | solution.py:494
  36.6 24.8 %collective-permute-start.6 = (f32[128,2048]{1,0:T(8,128)S(1)}, f32[128,2048]{1,0:T(8,128)S(1)}, u32[]{:S(2)}, u32[]{:S(2)}) collective-permute-start(f32[128,2048]{1,0:T(8,128)S(1)} %get-tuple-element.53), channel_id=1, source_target_pairs={{0,140},{1,141},{2,142},{3,143},{4,8},{5,9},{6,10},{7,11},{8,4},{9... | collective-permute-start | bytes 3145736 | tf_op jit(solution)/shard_map/ppermute | solution.py:498
  37.1 24.3 %collective-permute-start.5 = (f32[128,2048]{1,0:T(8,128)S(1)}, f32[128,2048]{1,0:T(8,128)S(1)}, u32[]{:S(2)}, u32[]{:S(2)}) collective-permute-start(f32[128,2048]{1,0:T(8,128)S(1)} %collective-permute-done.a_ref), channel_id=1, source_target_pairs={{0,32},{16,48},{32,0},{48,16},{64,96},{80,112},{96,64},{112,80},{1... | collective-permute-start | bytes 3145736 | tf_op jit(solution)/shard_map/ppermute | solution.py:494
  37.9 23.5 %collective-permute-start.7 = (f32[128,2048]{1,0:T(8,128)S(1)}, f32[128,2048]{1,0:T(8,128)S(1)}, u32[]{:S(2)}, u32[]{:S(2)}) collective-permute-start(f32[128,2048]{1,0:T(8,128)S(1)} %collective-permute-done.a_ref), channel_id=1, source_target_pairs={{0,96},{16,112},{32,64},{48,80},{64,32},{80,48},{96,0},{112,16},{1... | collective-permute-start | bytes 3145736 | tf_op jit(solution)/shard_map/ppermute | solution.py:494
  43.0 11.2 %collective-permute-start.9 = (f32[24,1024]{1,0:T(8,128)S(1)}, f32[24,1024]{1,0:T(8,128)S(1)}, u32[]{:S(2)}, u32[]{:S(2)}) collective-permute-start(f32[24,1024]{1,0:T(8,128)S(1)} %get-tuple-element.57), channel_id=1, source_target_pairs={{0,12},{1,13},{2,14},{3,15},{4,8},{5,9},{6,10},{7,11},{8,4},{9,5},... | collective-permute-start | bytes 294920 | tf_op jit(solution)/shard_map/ppermute | solution.py:494
  53.6 7.8 %collective-permute-start.12 = (f32[16,128]{1,0:T(8,128)S(1)}, f32[16,128]{1,0:T(8,128)S(1)}, u32[]{:S(2)}, u32[]{:S(2)}) collective-permute-start(f32[16,128]{1,0:T(8,128)S(1)} %add.24.d0), channel_id=1, source_target_pairs={{0,8},{1,9},{2,10},{3,11},{4,12},{5,13},{6,14},{7,15},{8,0},{9,1},... | collective-permute-start | bytes 24584 | tf_op jit(solution)/shard_map/ppermute | solution.py:494
  54.2 14.9 %collective-permute-start.13 = (f32[128,2048]{1,0:T(8,128)S(1)}, f32[128,2048]{1,0:T(8,128)S(1)}, u32[]{:S(2)}, u32[]{:S(2)}) collective-permute-start(f32[128,2048]{1,0:T(8,128)S(1)} %collective-permute-done.a_ref), channel_id=1, source_target_pairs={{0,16},{16,0},{32,48},{48,32},{64,80},{80,64},{96,112},{112,96},{1... | collective-permute-start | bytes 3145736 | tf_op jit(solution)/shard_map/ppermute | solution.py:494
  61.4 7.6 %collective-permute-start.14 = (f32[128,2048]{1,0:T(8,128)S(1)}, f32[128,2048]{1,0:T(8,128)S(1)}, u32[]{:S(2)}, u32[]{:S(2)}) collective-permute-start(f32[128,2048]{1,0:T(8,128)S(1)} %collective-permute-done.5.b_ref), channel_id=1, source_target_pairs={{0,16},{16,0},{32,48},{48,32},{64,80},{80,64},{96,112},{112,96},{1... | collective-permute-start | bytes 3145736 | tf_op jit(solution)/shard_map/ppermute | solution.py:494
  61.5 7.6 %collective-permute-start.15 = (f32[128,2048]{1,0:T(8,128)S(1)}, f32[128,2048]{1,0:T(8,128)S(1)}, u32[]{:S(2)}, u32[]{:S(2)}) collective-permute-start(f32[128,2048]{1,0:T(8,128)S(1)} %collective-permute-done.6.c_ref), channel_id=1, source_target_pairs={{0,16},{16,0},{32,48},{48,32},{64,80},{80,64},{96,112},{112,96},{1... | collective-permute-start | bytes 3145736 | tf_op jit(solution)/shard_map/ppermute | solution.py:494
  62.0 7.1 %collective-permute-start.16 = (f32[128,2048]{1,0:T(8,128)S(1)}, f32[128,2048]{1,0:T(8,128)S(1)}, u32[]{:S(2)}, u32[]{:S(2)}) collective-permute-start(f32[128,2048]{1,0:T(8,128)S(1)} %collective-permute-done.7.d_ref), channel_id=1, source_target_pairs={{0,16},{16,0},{32,48},{48,32},{64,80},{80,64},{96,112},{112,96},{1... | collective-permute-start | bytes 3145736 | tf_op jit(solution)/shard_map/ppermute | solution.py:494
  73.0 12.1 %collective-permute-start.17 = (f32[2,88,512]{2,1,0:T(8,128)S(1)}, f32[2,88,512]{2,1,0:T(8,128)S(1)}, u32[]{:S(2)}, u32[]{:S(2)}) collective-permute-start(f32[2,88,512]{2,1,0:T(8,128)S(1)} %get-tuple-element.73), channel_id=1, source_target_pairs={{0,1},{1,2},{2,3},{3,0},{4,5},{5,6},{6,7},{7,4},{8,9},{9,10},{10,1... | collective-permute-start | bytes 1081352 | tf_op jit(solution)/shard_map/ppermute | solution.py:490
  74.6 10.9 %collective-permute-start.19 = (f32[2,88,512]{2,1,0:T(8,128)S(1)}, f32[2,88,512]{2,1,0:T(8,128)S(1)}, u32[]{:S(2)}, u32[]{:S(2)}) collective-permute-start(f32[2,88,512]{2,1,0:T(8,128)S(1)} %get-tuple-element.78), channel_id=1, source_target_pairs={{0,3},{1,0},{2,1},{3,2},{4,7},{5,4},{6,5},{7,6},{8,11},{9,8},{10,9... | collective-permute-start | bytes 1081352 | tf_op jit(solution)/shard_map/ppermute | solution.py:490
  77.7 19.8 %collective-permute-start.21 = (f32[8,48,512]{2,1,0:T(8,128)S(1)}, f32[8,48,512]{2,1,0:T(8,128)S(1)}, u32[]{:S(2)}, u32[]{:S(2)}) collective-permute-start(f32[8,48,512]{2,1,0:T(8,128)S(1)} %gradient.6), channel_id=1, source_target_pairs={{0,4},{1,5},{2,6},{3,7},{4,0},{5,1},{6,2},{7,3},{8,12},{9,13},{10,... | collective-permute-start | bytes 2359304 | tf_op jit(solution)/shard_map/ppermute | solution.py:494
  85.1 19.0 %collective-permute-start.18 = (f32[4,88,512]{2,1,0:T(8,128)S(1)}, f32[4,88,512]{2,1,0:T(8,128)S(1)}, u32[]{:S(2)}, u32[]{:S(2)}) collective-permute-start(f32[4,88,512]{2,1,0:T(8,128)S(1)} %add_into.4), channel_id=1, source_target_pairs={{0,1},{1,2},{2,3},{3,0},{4,5},{5,6},{6,7},{7,4},{8,9},{9,10},{10,1... | collective-permute-start | bytes 2162696 | tf_op jit(solution)/shard_map/ppermute | solution.py:490
  85.6 18.5 %collective-permute-start.20 = (f32[4,88,512]{2,1,0:T(8,128)S(1)}, f32[4,88,512]{2,1,0:T(8,128)S(1)}, u32[]{:S(2)}, u32[]{:S(2)}) collective-permute-start(f32[4,88,512]{2,1,0:T(8,128)S(1)} %add_into.5), channel_id=1, source_target_pairs={{0,3},{1,0},{2,1},{3,2},{4,7},{5,4},{6,5},{7,6},{8,11},{9,8},{10,9... | collective-permute-start | bytes 2162696 | tf_op jit(solution)/shard_map/ppermute | solution.py:490
  104.3 9.6 %collective-permute-start.22 = (f32[2,88,512]{2,1,0:T(8,128)S(1)}, f32[2,88,512]{2,1,0:T(8,128)S(1)}, u32[]{:S(2)}, u32[]{:S(2)}) collective-permute-start(f32[2,88,512]{2,1,0:T(8,128)S(1)} %get-tuple-element.86), channel_id=1, source_target_pairs={{0,4},{1,5},{2,6},{3,7},{4,0},{5,1},{6,2},{7,3},{8,12},{9,13},{10,... | collective-permute-start | bytes 1081352 | tf_op jit(solution)/shard_map/ppermute | solution.py:494
  104.6 5.8 %collective-permute-start.24 = (f32[1,48,512]{2,1,0:T(8,128)S(1)}, f32[1,48,512]{2,1,0:T(8,128)S(1)}, u32[]{:S(2)}, u32[]{:S(2)}) collective-permute-start(f32[1,48,512]{2,1,0:T(8,128)S(1)} %get-tuple-element.80), channel_id=1, source_target_pairs={{0,1},{1,2},{2,3},{3,0},{4,5},{5,6},{6,7},{7,4},{8,9},{9,10},{10,1... | collective-permute-start | bytes 294920 | tf_op jit(solution)/shard_map/ppermute | solution.py:490
  105.1 5.4 %collective-permute-start.25 = (f32[1,48,512]{2,1,0:T(8,128)S(1)}, f32[1,48,512]{2,1,0:T(8,128)S(1)}, u32[]{:S(2)}, u32[]{:S(2)}) collective-permute-start(f32[1,48,512]{2,1,0:T(8,128)S(1)} %get-tuple-element.81), channel_id=1, source_target_pairs={{0,3},{1,0},{2,1},{3,2},{4,7},{5,4},{6,5},{7,6},{8,11},{9,8},{10,9... | collective-permute-start | bytes 294920 | tf_op jit(solution)/shard_map/ppermute | solution.py:490
  110.4 7.0 %collective-permute-start.26 = (f32[2,48,512]{2,1,0:T(8,128)S(1)}, f32[2,48,512]{2,1,0:T(8,128)S(1)}, u32[]{:S(2)}, u32[]{:S(2)}) collective-permute-start(f32[2,48,512]{2,1,0:T(8,128)S(1)} %add_into.6), channel_id=1, source_target_pairs={{0,1},{1,2},{2,3},{3,0},{4,5},{5,6},{6,7},{7,4},{8,9},{9,10},{10,1... | collective-permute-start | bytes 589832 | tf_op jit(solution)/shard_map/ppermute | solution.py:490
  111.8 5.8 %collective-permute-start.27 = (f32[2,48,512]{2,1,0:T(8,128)S(1)}, f32[2,48,512]{2,1,0:T(8,128)S(1)}, u32[]{:S(2)}, u32[]{:S(2)}) collective-permute-start(f32[2,48,512]{2,1,0:T(8,128)S(1)} %add_into.7), channel_id=1, source_target_pairs={{0,3},{1,0},{2,1},{3,2},{4,7},{5,4},{6,5},{7,6},{8,11},{9,8},{10,9... | collective-permute-start | bytes 589832 | tf_op jit(solution)/shard_map/ppermute | solution.py:490
  113.9 10.3 %collective-permute-start.23 = (f32[1,88,512]{2,1,0:T(8,128)S(1)}, f32[1,88,512]{2,1,0:T(8,128)S(1)}, u32[]{:S(2)}, u32[]{:S(2)}) collective-permute-start(f32[1,88,512]{2,1,0:T(8,128)S(1)} %get-tuple-element.88), channel_id=1, source_target_pairs={{0,12},{1,13},{2,14},{3,15},{4,8},{5,9},{6,10},{7,11},{8,4},{9,5},... | collective-permute-start | bytes 540680 | tf_op jit(solution)/shard_map/ppermute | solution.py:494
  117.6 6.6 %collective-permute-start.28 = (f32[1,48,512]{2,1,0:T(8,128)S(1)}, f32[1,48,512]{2,1,0:T(8,128)S(1)}, u32[]{:S(2)}, u32[]{:S(2)}) collective-permute-start(f32[1,48,512]{2,1,0:T(8,128)S(1)} %get-tuple-element.95), channel_id=1, source_target_pairs={{0,12},{1,13},{2,14},{3,15},{4,8},{5,9},{6,10},{7,11},{8,4},{9,5},... | collective-permute-start | bytes 294920 | tf_op jit(solution)/shard_map/ppermute | solution.py:494
  (10 other events, 101.3 us)
